TPU v7x, 32 devices: a whole 2x2x4 slice. The times are simulated.
32 devices in a mesh: dp: 8 (over z, x), tensor: 4 (over y, core).
Axes of the slice: x: 2, y: 2, z: 4, core: 2. Of those that a mesh axis runs over, the one named last changes fastest.
Arguments:
- inputs: bfloat16 [256, 8192], P('dp'), may hold values from -6 to 6
- gate_weight: bfloat16 [8192, 28, 1024], P('dp', None, 'tensor'), may hold values from -0.0625 to 0.0625
- up_weight: bfloat16 [8192, 28, 1024], P('dp', None, 'tensor'), may hold values from -0.0625 to 0.0625
- down_weight: bfloat16 [28, 1024, 8192], P(None, 'tensor', 'dp'), may hold values from -0.03125 to 0.03125
Outputs:
- mixed: float32 [256, 8192], P('tensor', 'dp')
All inputs are finite; a program needn't handle non-finite values.
Results may differ from a plain program's by a relative error of at most 0.0029.
Values may be sent and summed in bfloat16 or wider, within the bound.
A program may use at most 192 MiB of HBM per device.

v0:
```python
import math

import jax
import jax.numpy as jnp
import numpy as np
from jax import lax
from jax.sharding import PartitionSpec as P


def from_partner(value, axis, apart):
    mask = 2**apart
    pairs = [(source, source ^ mask) for source in range(lax.axis_size(axis))]
    return lax.ppermute(value, axis, pairs)


def sylvester_table(order):
    index = np.arange(order)
    common = index[:, None] & index[None, :]
    parity = np.zeros((order, order), np.int64)
    for level in range(max(order.bit_length(), 1)):
        parity = parity ^ common >> level & 1
    return (1 - 2 * parity).astype(np.float32)


def paley_table():
    prime = 13
    residues = [base_value * base_value % prime for base_value in range(1, prime)]
    jacobsthal = np.zeros((prime, prime), np.float32)
    for row_index in range(prime):
        for col_index in range(prime):
            offset = (col_index - row_index) % prime
            if offset != 0:
                jacobsthal[row_index, col_index] = 1.0 if offset in residues else -1.0
    conference = np.zeros((prime + 1, prime + 1), np.float32)
    conference[0, 1:] = 1.0
    conference[1:, 0] = 1.0
    conference[1:, 1:] = jacobsthal
    upper_block = np.array([[1.0, 1.0], [1.0, -1.0]], np.float32)
    lower_block = np.array([[1.0, -1.0], [-1.0, -1.0]], np.float32)
    return (
        np.kron(conference, upper_block) + np.kron(np.eye(prime + 1, dtype=np.float32), lower_block)
    ).astype(np.float32)


def per_device(inputs, gate_weight, up_weight, down_weight):
    local_depth, kernel_a, block_e = gate_weight.shape
    own_rows = inputs.shape[0]
    columns = lax.all_to_all(inputs, "dp", split_axis=1, concat_axis=0, tiled=True)
    gate_flat = gate_weight.reshape(local_depth, kernel_a * block_e)
    up_flat = up_weight.reshape(local_depth, kernel_a * block_e)
    joined = jnp.concatenate((gate_flat, up_flat), axis=1)
    summed = lax.psum_scatter(
        jnp.dot(columns, joined, preferred_element_type=jnp.float32),
        "dp",
        scatter_dimension=0,
        tiled=True,
    )
    split_at = kernel_a * block_e
    gate = summed[:, :split_at]
    upward = summed[:, split_at:]
    hidden = (jax.nn.silu(gate) * upward).reshape(own_rows, kernel_a, block_e)
    local_table = jnp.asarray(sylvester_table(block_e))
    turned = jnp.einsum("rae,ef->raf", hidden, local_table, precision=lax.Precision.HIGHEST)
    paley = jnp.asarray(paley_table()).astype(jnp.float32)
    turned = jnp.einsum("rak,ab->rbk", turned, paley, precision=lax.Precision.HIGHEST)
    groups = lax.axis_size("tensor")
    position = lax.axis_index("tensor")
    for level in range(groups.bit_length() - 1):
        partner = from_partner(turned, "tensor", level)
        upper = position >> level & 1 == 1
        turned = jnp.where(upper, partner - turned, turned + partner)
    rotated = (turned / math.sqrt(kernel_a * block_e * groups)).astype(jnp.bfloat16)
    down_flat = down_weight.reshape(kernel_a * block_e, down_weight.shape[2])
    piece = lax.all_gather(rotated, "dp", axis=0, tiled=True)
    partial_sums = jnp.dot(
        piece.reshape(piece.shape[0], kernel_a * block_e),
        down_flat,
        preferred_element_type=jnp.float32,
    )
    return lax.psum_scatter(partial_sums, "tensor", scatter_dimension=0, tiled=True)


def solution(mesh):
    return jax.shard_map(
        per_device,
        mesh=mesh,
        in_specs=(
            P("dp", None),
            P("dp", None, "tensor"),
            P("dp", None, "tensor"),
            P(None, "tensor", "dp"),
        ),
        out_specs=P("tensor", "dp"),
        check_vma=False,
    )
```

profile of v0, /device:TPU:0, one launch (start us, length us, event | category | flops | bytes accessed | tf_op | source)
XLA Modules:
  0.0 480.3 jit_solution(6327590503217660979)
XLA Ops:
  6.5 1.9 copy.48
  8.4 7.3 %all-to-all-start = ((bf16[32,8,1024]{2,0,1:T(8,128)(2,1)}), bf16[32,8,1024]{2,0,1:T(8,128)(2,1)S(1)}, u32[]{:S(2)}, u32[]{:S(2)}) async-start(bf16[32,8,1024]{2,0,1:T(8,128)(2,1)} %bitcast.27), calls=%async_computation | async-start | bytes 1048576 | tf_op jit(solution)/shard_map/all_to_all | solution.py:48
  15.7 0.0 reduce-scatter.7.cloned.1.call-start
  15.7 20.2 %copy.29 = bf16[1024,28,256]{0,2,1:T(8,128)(2,1)} copy(bf16[1024,28,256]{2,0,1:T(8,128)(2,1)} %param.7) | data formatting | bytes 29360128 | tf_op args[1]
  35.9 20.3 %copy.30 = bf16[1024,28,256]{0,2,1:T(8,128)(2,1)} copy(bf16[1024,28,256]{2,0,1:T(8,128)(2,1)} %param.8) | data formatting | bytes 29360128 | tf_op args[2]
  56.3 0.0 all-to-all-done
  56.3 18.2 %fusion.4 = f32[256,14336]{0,1:T(8,128)} fusion(bf16[256,1024]{1,0:T(8,128)(2,1)S(1)} %bitcast.33, bf16[1024,7168]{0,1:T(8,128)(2,1)} %bitcast.29, bf16[1024,7168]{0,1:T(8,128)(2,1)} %bitcast.28), kind=kOutput, calls=%fused_computation.4 | convolution fusion | flops 7574913024 | bytes 44564480 | tf_op jit(solution)/shard_map/dot_general | solution.py:53
  74.5 15.0 %copy.36 = f32[256,14336]{1,0:T(8,128)} copy(f32[256,14336]{0,1:T(8,128)} %fusion.4) | data formatting | bytes 29360128
  89.5 0.0 reduce-scatter.7.cloned.1.call-update
  89.5 0.0 copy-start
  89.5 0.0 copy-start.1
  89.6 0.2 all-gather.2.cloned.1.call-start
  89.8 237.8 %reduce-scatter.7.cloned.1.call-done = f32[32,14336]{1,0:T(8,128)} async-done(((f32[256,14336]{1,0:T(8,128)}), f32[32,14336]{1,0:T(8,128)}) %reduce-scatter.7.cloned.1.call-update) | async-done | bytes 1835024
  327.6 1.6 fusion.10
  329.2 2.4 copy.38
  331.6 2.4 copy.39
  334.1 4.1 multiply_multiply_fusion
  338.2 0.0 copy-done
  338.2 6.0 %fusion.11 = f32[32,28,256]{2,0,1:T(8,128)S(1)} fusion(f32[32,28,256]{0,2,1:T(8,128)S(1)} %bitcast.30, f32[256,256,1]{1,0,2:T(8,128)S(1)} %copy-done), kind=kOutput, calls=%fused_computation.15 | convolution fusion | flops 704643072 | bytes 2097152 | tf_op jit(solution)/shard_map/rae,ef->raf/dot_general | solution.py:63
  344.2 0.0 copy-done.1
  344.2 1.6 fusion.7
  345.9 0.5 copy.47
  346.4 0.1 collective-permute-start
  346.5 2.5 collective-permute-done
  348.9 0.6 add_select_fusion
  349.5 1.6 collective-permute-start.1
  351.1 20.9 %collective-permute-done.1 = f32[32,28,256]{2,0,1:T(8,128)S(1)} collective-permute-done((f32[32,28,256]{2,0,1:T(8,128)S(1)}, f32[32,28,256]{2,0,1:T(8,128)S(1)}, u32[]{:S(2)}, u32[]{:S(2)}) %collective-permute-start.1) | collective-permute-done | bytes 917536 | tf_op jit(solution)/shard_map/ppermute | solution.py:13
  372.0 1.0 multiply_convert_fusion
  372.9 0.0 all-gather.2.cloned.1.call-update
  373.0 0.3 reduce-scatter.5.cloned.1.call-start
  373.2 65.8 %all-gather.2.cloned.1.call-done = bf16[256,28,256]{2,0,1:T(8,128)(2,1)} async-done(((bf16[32,28,256]{2,0,1:T(8,128)(2,1)}), bf16[256,28,256]{2,0,1:T(8,128)(2,1)}) %all-gather.2.cloned.1.call-update) | async-done | bytes 3670032 | tf_op jit(solution)/shard_map/all_gather | solution.py:74
  439.0 11.2 %convolution_bitcast_fusion = f32[256,1024]{1,0:T(8,128)} fusion(bf16[256,28,256]{2,0,1:T(8,128)(2,1)} %all-gather.2.cloned.1.call-done, bf16[28,256,1024]{2,1,0:T(8,128)(2,1)} %param.9), kind=kOutput, calls=%fused_computation.6 | convolution fusion | flops 3758096384 | bytes 19398656 | tf_op jit(solution)/shard_map/dot_general | solution.py:75
  450.3 0.0 reduce-scatter.5.cloned.1.call-update
  450.3 23.5 %reduce-scatter.5.cloned.1.call-done = f32[64,1024]{1,0:T(8,128)} async-done(((f32[256,1024]{1,0:T(8,128)}), f32[64,1024]{1,0:T(8,128)}) %reduce-scatter.5.cloned.1.call-update) | async-done | bytes 262160 | tf_op jit(solution)/shard_map/reduce_scatter | solution.py:80
Async XLA Ops:
  8.4 47.8 %all-to-all-start = ((bf16[32,8,1024]{2,0,1:T(8,128)(2,1)}), bf16[32,8,1024]{2,0,1:T(8,128)(2,1)S(1)}, u32[]{:S(2)}, u32[]{:S(2)}) async-start(bf16[32,8,1024]{2,0,1:T(8,128)(2,1)} %bitcast.27), calls=%async_computation | async-start | bytes 1048576 | tf_op jit(solution)/shard_map/all_to_all | solution.py:48
  15.7 311.9 %reduce-scatter.7.cloned.1.call-start = ((), (), s32[]{:S(2)}) async-start(), calls=%async_computation.5 | async-start | bytes 16515072
  89.5 248.7 %copy-start = (f32[256,256,1]{1,0,2:T(8,128)S(1)}, f32[256,256,1]{1,0,2:T(8,128)}, u32[]{:S(2)}) copy-start(f32[256,256,1]{1,0,2:T(8,128)} %constant.20) | copy-start | bytes 786436
  89.5 254.7 %copy-start.1 = (f32[28,28,1]{0,1,2:T(8,128)S(1)}, f32[28,28,1]{0,1,2:T(8,128)}, u32[]{:S(2)}) copy-start(f32[28,28,1]{0,1,2:T(8,128)} %constant.21) | copy-start | bytes 9412
  89.6 349.5 %all-gather.2.cloned.1.call-start = ((), (), s32[]{:S(2)}) async-start(), calls=%async_computation.3 | async-start | bytes 4128768 | tf_op jit(solution)/shard_map/all_gather | solution.py:74
  346.4 2.5 collective-permute-start
  349.5 22.5 %collective-permute-start.1 = (f32[32,28,256]{2,0,1:T(8,128)S(1)}, f32[32,28,256]{2,0,1:T(8,128)S(1)}, u32[]{:S(2)}, u32[]{:S(2)}) collective-permute-start(f32[32,28,256]{2,0,1:T(8,128)S(1)} %add_select_fusion), channel_id=1, source_target_pairs={{0,2},{1,3},{2,0},{3,1},{4,6},{5,7},{6,4},{7,5},{8,10},{9,11},{10,... | collective-permute-start | bytes 2752520 | tf_op jit(solution)/shard_map/ppermute | solution.py:13
  373.0 100.8 %reduce-scatter.5.cloned.1.call-start = ((), (), s32[]{:S(2)}) async-start(), calls=%async_computation.4 | async-start | bytes 1310720 | tf_op jit(solution)/shard_map/reduce_scatter | solution.py:80
Sparse Core Ops, SparseCore 0:
  89.7 237.9 reduce-scatter.6
  373.1 65.9 all-gather.1
  450.4 23.3 reduce-scatter.4
where the time goes:
time: 482 us; the launch traced here: 480 us
  waiting for transfers between devices  351 us (73%)
  local copies, waits for them, and re-layouts  64.5 us (13%)
  matrix products  37.1 us (8%)
  between operations  13.2 us (3%)
  starting transfers between devices  9.4 us (2%)
  other arithmetic  5.65 us (1%)
    unnamed x4, waiting for transfers between devices  238 us
    all_gather x1, waiting for transfers between devices, per_device(): piece = lax.all_gather(rotated, 'dp', axis=0, tiled=True)  65.8 us
    unnamed x9, local copies, waits for them, and re-layouts  60.4 us
    reduce_scatter x1, waiting for transfers between devices, per_device(): lax.psum_scatter(partial_sums, 'tensor', scatter_dimension=0, tiled=True)  23.5 us
    ppermute x2, waiting for transfers between devices, from_partner(): return lax.ppermute(value, axis, pairs)  23.4 us
    dot_general x1, matrix products, per_device(): jnp.dot(columns, joined, preferred_element_type=jnp.float32)  18.2 us
    dot_general x1, matrix products, per_device(): jnp.dot(piece.reshape(piece.shape[0], kernel_a * block_e), down_flat, pre...  11.2 us
  transfers between devices with their start and end apart: 6, of which 5 were waited for; matrix products, arithmetic and copies ran while one was open for 8% of the time, Pallas kernels for 0%

commit v1 on v0

v1 whole, which is shorter than its diff:
```python
import functools
import math

import jax
import jax.numpy as jnp
import numpy as np
from jax import lax
from jax.experimental import pallas as pl
from jax.experimental.pallas import tpu as pltpu
from jax.sharding import PartitionSpec as P

RING = 4
LAG = 2


def sylvester_table(order):
    index = np.arange(order)
    common = index[:, None] & index[None, :]
    parity = np.zeros((order, order), np.int64)
    for level in range(max(order.bit_length(), 1)):
        parity = parity ^ common >> level & 1
    return (1 - 2 * parity).astype(np.float32)


def paley_table():
    prime = 13
    residues = [base_value * base_value % prime for base_value in range(1, prime)]
    jacobsthal = np.zeros((prime, prime), np.float32)
    for row_index in range(prime):
        for col_index in range(prime):
            offset = (col_index - row_index) % prime
            if offset != 0:
                jacobsthal[row_index, col_index] = 1.0 if offset in residues else -1.0
    conference = np.zeros((prime + 1, prime + 1), np.float32)
    conference[0, 1:] = 1.0
    conference[1:, 0] = 1.0
    conference[1:, 1:] = jacobsthal
    upper_block = np.array([[1.0, 1.0], [1.0, -1.0]], np.float32)
    lower_block = np.array([[1.0, -1.0], [-1.0, -1.0]], np.float32)
    return (
        np.kron(conference, upper_block) + np.kron(np.eye(prime + 1, dtype=np.float32), lower_block)
    ).astype(np.float32)


def encode(value):
    square = value * value
    return (value * jnp.abs(value) * square).astype(jnp.bfloat16)


def decode(code):
    wide = code.astype(jnp.float32)
    root = lax.rsqrt(lax.rsqrt(jnp.abs(wide)))
    return jnp.where(wide < 0, -root, root)


def partner_of(axis, bit):
    me = lax.axis_index(axis)
    high = lax.rem(me // (1 << bit), 2)
    return me + (1 - 2 * high) * (1 << bit), high


def hidden_kernel(halvings, doublings, factor, *refs):
    x_ref, gate_ref, up_ref, table_ref, out_ref = refs[:5]
    rest = list(refs[5:])
    weights, part, turned = rest[:3]
    del rest[:3]
    sends, rest = rest[: halvings + doublings], rest[halvings + doublings :]
    arrivals, rest = rest[: halvings + doublings], rest[halvings + doublings :]
    keeps, rest = rest[:halvings], rest[halvings:]
    weight_sem, send_sem, recv_sem = rest
    count, _, block = gate_ref.shape
    rows = x_ref.shape[0]
    places = [("dp", bit) + partner_of("dp", bit) for bit in range(halvings)]
    places += [("tensor", bit) + partner_of("tensor", bit) for bit in range(doublings)]

    def fetch(chunk, slot):
        return [
            pltpu.make_async_copy(source.at[chunk], weights.at[slot, which], weight_sem.at[slot, which])
            for which, source in enumerate((gate_ref, up_ref))
        ]

    def transfer(stage, chunk):
        axis, _, partner, _ = places[stage]
        return pltpu.make_async_remote_copy(
            src_ref=sends[stage].at[chunk],
            dst_ref=arrivals[stage].at[chunk],
            send_sem=send_sem.at[stage, chunk],
            recv_sem=recv_sem.at[stage, chunk],
            device_id={axis: partner},
            device_id_type=pl.DeviceIdType.MESH,
        )

    for copy in fetch(0, 0):
        copy.start()
    barrier = pltpu.get_barrier_semaphore()
    for axis, _, partner, _ in places:
        pl.semaphore_signal(barrier, inc=1, device_id={axis: partner}, device_id_type=pl.DeviceIdType.MESH)
    pl.semaphore_wait(barrier, len(places))

    def multiply(chunk):
        slot = lax.rem(chunk, 2)

        @pl.when(chunk + 1 < count)
        def _():
            for copy in fetch(chunk + 1, 1 - slot):
                copy.start()

        for copy in fetch(chunk, slot):
            copy.wait()
        for which in range(2):
            part[:, which * block : (which + 1) * block] = jnp.dot(
                x_ref[...], weights[slot, which], preferred_element_type=jnp.float32
            )
        half = rows // 2
        high = places[0][3]
        theirs = pl.multiple_of((1 - high) * half, half)
        ours = pl.multiple_of(high * half, half)
        sends[0][chunk] = encode(part[pl.ds(theirs, half), :])
        transfer(0, chunk).start()
        keeps[0][lax.rem(chunk, RING)] = part[pl.ds(ours, half), :]

    def halve(stage, chunk):
        transfer(stage - 1, chunk).wait_recv()
        slot = lax.rem(chunk, RING)
        half = rows >> (stage + 1)
        high = places[stage][3]
        theirs = pl.ds(pl.multiple_of((1 - high) * half, half), half)
        ours = pl.ds(pl.multiple_of(high * half, half), half)
        sends[stage][chunk] = encode(keeps[stage - 1][slot, theirs, :] + decode(arrivals[stage - 1][chunk, theirs, :]))
        transfer(stage, chunk).start()
        keeps[stage][slot] = keeps[stage - 1][slot, ours, :] + decode(arrivals[stage - 1][chunk, ours, :])

    def activate(chunk):
        transfer(halvings - 1, chunk).wait_recv()
        both = keeps[halvings - 1][lax.rem(chunk, RING)] + decode(arrivals[halvings - 1][chunk])
        gate, upward = both[:, :block], both[:, block:]
        hidden = gate / (1.0 + jnp.exp(-gate)) * upward
        own = hidden.shape[0]
        first = hidden.astype(jnp.bfloat16)
        left = hidden - first.astype(jnp.float32)
        second = left.astype(jnp.bfloat16)
        third = (left - second.astype(jnp.float32)).astype(jnp.bfloat16)
        pieces = jnp.dot(
            jnp.concatenate((first, second, third), axis=0), table_ref[...], preferred_element_type=jnp.float32
        )
        store(halvings, chunk, pieces[:own] + pieces[own : 2 * own] + pieces[2 * own :])

    def store(stage, chunk, value):
        if stage == halvings + doublings:
            turned[chunk] = value
        else:
            sends[stage][chunk] = value
            transfer(stage, chunk).start()

    def butterfly(stage, chunk):
        transfer(stage, chunk).wait_recv()
        sign = (1 - 2 * places[stage][3]).astype(jnp.float32)
        store(stage + 1, chunk, sign * sends[stage][chunk] + arrivals[stage][chunk])

    steps = [multiply]
    steps += [functools.partial(halve, stage) for stage in range(1, halvings)]
    steps += [activate]
    steps += [functools.partial(butterfly, halvings + level) for level in range(doublings)]

    def iteration(turn, carry):
        for order, step in enumerate(steps):
            chunk = turn - order * LAG

            @pl.when((chunk >= 0) & (chunk < count))
            def _(step=step, chunk=chunk):
                step(chunk)

        return carry

    lax.fori_loop(0, count + (len(steps) - 1) * LAG, iteration, 0)

    paley = paley_table()
    scale = 1.0 / math.sqrt(factor)
    band = 16

    def mix(index, carry):
        place = pl.ds(pl.multiple_of(index * band, band), band)
        for lane in range(0, block, 128):
            values = [turned[a, place, lane : lane + 128] for a in range(count)]
            for b in range(count):
                total = values[0] if paley[0, b] > 0 else -values[0]
                for a in range(1, count):
                    total = total + values[a] if paley[a, b] > 0 else total - values[a]
                out_ref[place, b * block + lane : b * block + lane + 128] = (total * scale).astype(jnp.bfloat16)
        return carry

    lax.fori_loop(0, turned.shape[1] // band, mix, 0)

    def drain(chunk, carry):
        for stage in range(halvings + doublings):
            transfer(stage, chunk).wait_send()
        return carry

    lax.fori_loop(0, count, drain, 0)


def rotated_hidden(columns, gate_weight, up_weight, groups, tensor):
    depth, count, block = gate_weight.shape
    rows = columns.shape[0]
    halvings = groups.bit_length() - 1
    doublings = tensor.bit_length() - 1
    own = rows // groups
    shape = (2,) * halvings + (own, depth)
    order = tuple(range(halvings))[::-1] + (halvings, halvings + 1)
    columns = columns.reshape(shape).transpose(order).reshape(rows, depth)
    table = jnp.asarray(sylvester_table(block), jnp.bfloat16)
    halves = [pltpu.VMEM((count, rows >> (level + 1), 2 * block), jnp.bfloat16) for level in range(halvings)]
    wholes = [pltpu.VMEM((count, own, block), jnp.float32) for _ in range(doublings)]
    keeps = [pltpu.VMEM((RING, rows >> (level + 1), 2 * block), jnp.float32) for level in range(halvings)]
    stages = halvings + doublings
    vmem = pl.BlockSpec(memory_space=pltpu.VMEM)
    hbm = pl.BlockSpec(memory_space=pl.ANY)
    return pl.pallas_call(
        functools.partial(hidden_kernel, halvings, doublings, count * block * tensor),
        out_shape=jax.ShapeDtypeStruct((own, count * block), jnp.bfloat16),
        in_specs=[vmem, hbm, hbm, vmem],
        out_specs=vmem,
        scratch_shapes=[
            pltpu.VMEM((2, 2, depth, block), jnp.bfloat16),
            pltpu.VMEM((rows, 2 * block), jnp.float32),
            pltpu.VMEM((count, own, block), jnp.float32),
            *halves,
            *wholes,
            *halves,
            *wholes,
            *keeps,
            pltpu.SemaphoreType.DMA((2, 2)),
            pltpu.SemaphoreType.DMA((stages, count)),
            pltpu.SemaphoreType.DMA((stages, count)),
        ],
        compiler_params=pltpu.CompilerParams(collective_id=0, has_side_effects=True, vmem_limit_bytes=56 * 2**20),
        cost_estimate=pl.CostEstimate(
            flops=4 * rows * depth * count * block,
            bytes_accessed=4 * depth * count * block,
            transcendentals=4 * rows * count * block,
        ),
    )(columns, jnp.transpose(gate_weight, (1, 0, 2)), jnp.transpose(up_weight, (1, 0, 2)), table)


def per_device(groups, tensor, inputs, gate_weight, up_weight, down_weight):
    kernel_a, block_e, width = down_weight.shape
    columns = lax.all_to_all(inputs, "dp", split_axis=1, concat_axis=0, tiled=True)
    rotated = rotated_hidden(columns, gate_weight, up_weight, groups, tensor)
    piece = lax.all_gather(rotated, "dp", axis=0, tiled=True)
    partial_sums = jnp.dot(
        piece, down_weight.reshape(kernel_a * block_e, width), preferred_element_type=jnp.float32
    )
    return lax.psum_scatter(partial_sums, "tensor", scatter_dimension=0, tiled=True)


def solution(mesh):
    return jax.shard_map(
        functools.partial(per_device, mesh.shape["dp"], mesh.shape["tensor"]),
        mesh=mesh,
        in_specs=(
            P("dp", None),
            P("dp", None, "tensor"),
            P("dp", None, "tensor"),
            P(None, "tensor", "dp"),
        ),
        out_specs=P("tensor", "dp"),
        check_vma=False,
    )
```

time: 482 us -> 237 us (0.49)
  waiting for transfers between devices: 351 us -> 89.3 us
  Pallas kernels: 0 us -> 99.5 us
  local copies, waits for them, and re-layouts: 64.5 us -> 1.92 us
  matrix products: 37.1 us -> 11.2 us
  blocking collectives: 0 us -> 21.6 us
  starting transfers between devices: 9.4 us -> 0.04 us
  other arithmetic: 5.65 us -> 0 us
    unnamed x4 -> x2, waiting for transfers between devices: 238 us -> 0.03 us
    pallas_call x0 -> x1, Pallas kernels: none -> 99.5 us  [rotated_hidden(): pl.pallas_call(functools.partial(hidden_kernel, halvings, doublings, coun...]
    unnamed x9 -> x0, local copies, waits for them, and re-layouts: 60.4 us -> none
    dot_general x4 -> x1, matrix products: 37.1 us -> 11.2 us  [per_device(): jnp.dot(piece, down_weight.reshape(kernel_a * block_e, width), preferred_...]
    ppermute x2 -> x0, waiting for transfers between devices: 23.4 us -> none  [from_partner(): return lax.ppermute(value, axis, pairs)]
    all_to_all x0 -> x1, blocking collectives: none -> 21.6 us  [per_device(): lax.all_to_all(inputs, 'dp', split_axis=1, concat_axis=0, tiled=True)]
    all_to_all x1 -> x0, starting transfers between devices: 7.25 us -> none  [per_device(): lax.all_to_all(inputs, 'dp', split_axis=1, concat_axis=0, tiled=True)]
  transfers between devices with their start and end apart: 6 -> 2, of which waited for: 5 -> 2; matrix products, arithmetic and copies ran while one was open for 8% -> 0% of each run, Pallas kernels for 0% -> 0%
where the time goes in v1:
time: 237 us
  Pallas kernels  99.5 us (42%)
  waiting for transfers between devices  89.3 us (38%)
  blocking collectives  21.6 us (9%)
  between operations  13.4 us (6%)
  matrix products  11.2 us (5%)
    pallas_call x1, Pallas kernels, rotated_hidden(): pl.pallas_call(functools.partial(hidden_kernel, halvings, doublings, coun...  99.5 us
    all_gather x1, waiting for transfers between devices, per_device(): piece = lax.all_gather(rotated, 'dp', axis=0, tiled=True)  65.7 us
    reduce_scatter x1, waiting for transfers between devices, per_device(): lax.psum_scatter(partial_sums, 'tensor', scatter_dimension=0, tiled=True)  23.5 us
    all_to_all x1, blocking collectives, per_device(): lax.all_to_all(inputs, 'dp', split_axis=1, concat_axis=0, tiled=True)  21.6 us
    dot_general x1, matrix products, per_device(): jnp.dot(piece, down_weight.reshape(kernel_a * block_e, width), preferred_...  11.2 us
  transfers between devices with their start and end apart: 2, of which 2 were waited for; matrix products, arithmetic and copies ran while one was open for 0% of the time, Pallas kernels for 0%

profile of v1, /device:TPU:0, one launch (start us, length us, event | category | flops | bytes accessed | tf_op | source)
XLA Modules:
  0.0 237.0 jit_solution(14118580308031762905)
XLA Ops:
  6.5 0.0 all-gather.2.cloned.1.call-start
  6.5 1.1 copy.13
  7.6 21.6 %all_to_all.16 = bf16[32,8,1024]{2,0,1:T(8,128)(2,1)S(1)} all-to-all(bf16[32,8,1024]{2,0,1:T(8,128)(2,1)S(1)} %bitcast.18), channel_id=1, replica_groups=mesh['dp'=8,'tensor'=4] {'dp'}, dimensions={1} | all-to-all | bytes 1048576 | tf_op jit(solution)/shard_map/all_to_all | solution.py:247
  29.2 0.8 copy.10
  30.0 99.5 %shard_map.55 = bf16[32,7168]{1,0:T(8,128)(2,1)} custom-call(bf16[256,1024]{1,0:T(8,128)(2,1)} %bitcast.19, bf16[28,1024,256]{2,1,0:T(8,128)(2,1)} %bitcast.15, bf16[28,1024,256]{2,1,0:T(8,128)(2,1)} %bitcast.16, bf16[256,256]{1,0:T(8,128)(2,1)} %constant.2.clone.refs_3_), custom_call_target="tpu_custom_call" | custom-call | flops 7516192768 | bytes 29360128 | tf_op jit(solution)/shard_map/pallas_call | solution.py:218
  129.6 0.0 all-gather.2.cloned.1.call-update
  129.6 0.0 reduce-scatter.2.cloned.1.call-start
  129.7 65.7 %all-gather.2.cloned.1.call-done = bf16[256,7168]{1,0:T(8,128)(2,1)} async-done(((bf16[32,7168]{1,0:T(8,128)(2,1)}), bf16[256,7168]{1,0:T(8,128)(2,1)}) %all-gather.2.cloned.1.call-update) | async-done | bytes 3670032 | tf_op jit(solution)/shard_map/all_gather | solution.py:249
  195.4 11.2 %fusion = f32[256,1024]{1,0:T(8,128)} fusion(bf16[256,7168]{1,0:T(8,128)(2,1)} %all-gather.2.cloned.1.call-done, bf16[7168,1024]{1,0:T(8,128)(2,1)} %bitcast.21), kind=kOutput, calls=%fused_computation.1 | convolution fusion | flops 3758096384 | bytes 19398656 | tf_op jit(solution)/shard_map/dot_general | solution.py:250
  206.6 0.0 reduce-scatter.2.cloned.1.call-update
  206.7 23.5 %reduce-scatter.2.cloned.1.call-done = f32[64,1024]{1,0:T(8,128)} async-done(((f32[256,1024]{1,0:T(8,128)}), f32[64,1024]{1,0:T(8,128)}) %reduce-scatter.2.cloned.1.call-update) | async-done | bytes 262160 | tf_op jit(solution)/shard_map/reduce_scatter | solution.py:253
Async XLA Ops:
  6.5 188.9 %all-gather.2.cloned.1.call-start = ((), (), s32[]{:S(2)}) async-start(), calls=%async_computation.2 | async-start | bytes 4128768 | tf_op jit(solution)/shard_map/all_gather | solution.py:249
  129.6 100.5 %reduce-scatter.2.cloned.1.call-start = ((), (), s32[]{:S(2)}) async-start(), calls=%async_computation.3 | async-start | bytes 1310720 | tf_op jit(solution)/shard_map/reduce_scatter | solution.py:253
Sparse Core Ops, SparseCore 0:
  129.7 65.6 all-gather.1
  206.8 23.3 reduce-scatter.1

commit v2 on v1

--- a/solution.py
+++ b/solution.py
@@ -242,15 +242,183 @@
     )(columns, jnp.transpose(gate_weight, (1, 0, 2)), jnp.transpose(up_weight, (1, 0, 2)), table)
 
 
+def reversed_bits(axis, bits):
+    me = lax.axis_index(axis)
+    return sum(lax.rem(me // (1 << bit), 2) * (1 << (bits - 1 - bit)) for bit in range(bits))
+
+
+def down_kernel(levels, folds, span, *refs):
+    rotated_ref, down_ref, out_ref, gathered, weights, total = refs[:6]
+    rest = list(refs[6:])
+    sends, rest = rest[:folds], rest[folds:]
+    arrivals, rest = rest[:folds], rest[folds:]
+    keeps, rest = rest[:folds], rest[folds:]
+    weight_sem, send_sem, recv_sem, fold_send_sem, fold_recv_sem = rest
+    own = rotated_ref.shape[0]
+    rows, width = total.shape
+    chunks = gathered.shape[0]
+    groups = 1 << levels
+    block = out_ref.shape[0]
+    tiles = max(1, min(4, width // 128))
+    tile_width = width // tiles
+    place = reversed_bits("dp", levels)
+    spread = [partner_of("dp", levels - 1 - stage) for stage in range(levels)]
+    folded = [partner_of("tensor", level) for level in range(folds)]
+
+    def fetch(chunk):
+        source = down_ref.at[pl.ds(pl.multiple_of(chunk * span, span), span), :]
+        return pltpu.make_async_copy(source, weights.at[chunk], weight_sem.at[chunk])
+
+    def prefetch(chunk, carry):
+        fetch(chunk).start()
+        return carry
+
+    lax.fori_loop(0, chunks, prefetch, 0)
+    barrier = pltpu.get_barrier_semaphore()
+    for partner, _ in spread:
+        pl.semaphore_signal(barrier, inc=1, device_id={"dp": partner}, device_id_type=pl.DeviceIdType.MESH)
+    for partner, _ in folded:
+        pl.semaphore_signal(barrier, inc=1, device_id={"tensor": partner}, device_id_type=pl.DeviceIdType.MESH)
+    mine = pl.ds(pl.multiple_of(place * own, own), own)
+    for chunk in range(chunks):
+        gathered[chunk, mine, :] = rotated_ref[:, chunk * span : (chunk + 1) * span]
+    pl.semaphore_wait(barrier, levels + folds)
+
+    def transfer(stage, chunk):
+        size = own << stage
+        start = place // (1 << stage) * size
+        held = gathered.at[chunk, pl.ds(pl.multiple_of(start, size), size), :]
+        return pltpu.make_async_remote_copy(
+            src_ref=held,
+            dst_ref=held,
+            send_sem=send_sem.at[stage, chunk],
+            recv_sem=recv_sem.at[stage, chunk],
+            device_id={"dp": spread[stage][0]},
+            device_id_type=pl.DeviceIdType.MESH,
+        )
+
+    def relay(stage, chunk):
+        if stage > 0:
+            transfer(stage - 1, chunk).wait_recv()
+        transfer(stage, chunk).start()
+
+    def natural(block_index):
+        return sum((block_index >> bit & 1) << (levels - 1 - bit) for bit in range(levels))
+
+    def multiply(chunk):
+        transfer(levels - 1, chunk).wait_recv()
+        fetch(chunk).wait()
+        left = jnp.concatenate(
+            [gathered[chunk, natural(p) * own : (natural(p) + 1) * own, :] for p in range(groups)], axis=0
+        )
+        for tile in range(tiles):
+            cols = slice(tile * tile_width, (tile + 1) * tile_width)
+            total[:, cols] += jnp.dot(left, weights[chunk, :, cols], preferred_element_type=jnp.float32)
+
+    total[...] = jnp.zeros_like(total)
+    steps = [functools.partial(relay, stage) for stage in range(levels)] + [multiply]
+
+    def iteration(turn, carry):
+        for order, step in enumerate(steps):
+            chunk = turn - order * LAG
+
+            @pl.when((chunk >= 0) & (chunk < chunks))
+            def _(step=step, chunk=chunk):
+                step(chunk)
+
+        return carry
+
+    lax.fori_loop(0, chunks + (len(steps) - 1) * LAG, iteration, 0)
+
+    def fold(level, tile):
+        cols = pl.ds(tile * tile_width, tile_width)
+        return pltpu.make_async_remote_copy(
+            src_ref=sends[level].at[:, cols],
+            dst_ref=arrivals[level].at[:, cols],
+            send_sem=fold_send_sem.at[level, tile],
+            recv_sem=fold_recv_sem.at[level, tile],
+            device_id={"tensor": folded[level][0]},
+            device_id_type=pl.DeviceIdType.MESH,
+        )
+
+    def part_of(level, index, bit):
+        source = total if level == 0 else keeps[level - 1]
+        return source, pl.ds(pl.multiple_of((2 * index + bit) * block, block), block)
+
+    def give(level, tile):
+        cols = slice(tile * tile_width, (tile + 1) * tile_width)
+        for index in range(1 << (folds - 1 - level)):
+            source, at = part_of(level, index, 1 - folded[level][1])
+            sends[level][index * block : (index + 1) * block, cols] = source[at, cols]
+        fold(level, tile).start()
+
+    for tile in range(tiles):
+        give(0, tile)
+    for level in range(folds):
+        for tile in range(tiles):
+            cols = slice(tile * tile_width, (tile + 1) * tile_width)
+            fold(level, tile).wait_recv()
+            target = out_ref if level + 1 == folds else keeps[level]
+            for index in range(1 << (folds - 1 - level)):
+                source, at = part_of(level, index, folded[level][1])
+                span_of = slice(index * block, (index + 1) * block)
+                target[span_of, cols] = source[at, cols] + arrivals[level][span_of, cols]
+            if level + 1 < folds:
+                give(level + 1, tile)
+
+    def drain(chunk, carry):
+        for stage in range(levels):
+            transfer(stage, chunk).wait_send()
+        return carry
+
+    lax.fori_loop(0, chunks, drain, 0)
+    for level in range(folds):
+        for tile in range(tiles):
+            fold(level, tile).wait_send()
+
+
+def mixed_rows(rotated, down_flat, count, groups, tensor):
+    own, hidden = rotated.shape
+    width = down_flat.shape[1]
+    rows = own * groups
+    levels = groups.bit_length() - 1
+    folds = tensor.bit_length() - 1
+    chunks = count // 2
+    span = hidden // chunks
+    block = rows // tensor
+    tiles = max(1, min(4, width // 128))
+    halves = [pltpu.VMEM((rows >> (level + 1), width), jnp.float32) for level in range(folds)]
+    vmem = pl.BlockSpec(memory_space=pltpu.VMEM)
+    return pl.pallas_call(
+        functools.partial(down_kernel, levels, folds, span),
+        out_shape=jax.ShapeDtypeStruct((block, width), jnp.float32),
+        in_specs=[vmem, pl.BlockSpec(memory_space=pl.ANY)],
+        out_specs=vmem,
+        scratch_shapes=[
+            pltpu.VMEM((chunks, rows, span), jnp.bfloat16),
+            pltpu.VMEM((chunks, span, width), jnp.bfloat16),
+            pltpu.VMEM((rows, width), jnp.float32),
+            *halves,
+            *halves,
+            *halves,
+            pltpu.SemaphoreType.DMA((chunks,)),
+            pltpu.SemaphoreType.DMA((levels, chunks)),
+            pltpu.SemaphoreType.DMA((levels, chunks)),
+            pltpu.SemaphoreType.DMA((folds, tiles)),
+            pltpu.SemaphoreType.DMA((folds, tiles)),
+        ],
+        compiler_params=pltpu.CompilerParams(collective_id=1, has_side_effects=True, vmem_limit_bytes=56 * 2**20),
+        cost_estimate=pl.CostEstimate(
+            flops=2 * rows * hidden * width, bytes_accessed=2 * hidden * width, transcendentals=0
+        ),
+    )(rotated, down_flat)
+
+
 def per_device(groups, tensor, inputs, gate_weight, up_weight, down_weight):
     kernel_a, block_e, width = down_weight.shape
     columns = lax.all_to_all(inputs, "dp", split_axis=1, concat_axis=0, tiled=True)
     rotated = rotated_hidden(columns, gate_weight, up_weight, groups, tensor)
-    piece = lax.all_gather(rotated, "dp", axis=0, tiled=True)
-    partial_sums = jnp.dot(
-        piece, down_weight.reshape(kernel_a * block_e, width), preferred_element_type=jnp.float32
-    )
-    return lax.psum_scatter(partial_sums, "tensor", scatter_dimension=0, tiled=True)
+    return mixed_rows(rotated, down_weight.reshape(kernel_a * block_e, width), kernel_a, groups, tensor)
 
 
 def solution(mesh):

time: 237 us -> 186 us (0.78)
  waiting for transfers between devices: 89.3 us -> 0 us
  Pallas kernels: 99.5 us -> 160 us
  between operations: 13.4 us -> 0.02 us
  matrix products: 11.2 us -> 0 us
    all_gather x1 -> x0, waiting for transfers between devices: 65.7 us -> none  [per_device(): piece = lax.all_gather(rotated, 'dp', axis=0, tiled=True)]
    pallas_call x0 -> x1, Pallas kernels: none -> 60.4 us  [mixed_rows(): pl.pallas_call(functools.partial(down_kernel, levels, folds, span), out_s...]
    reduce_scatter x1 -> x0, waiting for transfers between devices: 23.5 us -> none  [per_device(): lax.psum_scatter(partial_sums, 'tensor', scatter_dimension=0, tiled=True)]
    dot_general x1 -> x0, matrix products: 11.2 us -> none  [per_device(): jnp.dot(piece, down_weight.reshape(kernel_a * block_e, width), preferred_...]
  transfers between devices with their start and end apart: 2 -> 0, of which waited for: 2 -> 0; matrix products, arithmetic and copies ran while one was open for 0% -> 0% of each run, Pallas kernels for 0% -> 0%
where the time goes in v2:
time: 186 us; the launch traced here: 185 us
  Pallas kernels  160 us (86%)
  blocking collectives  21.6 us (12%)
  local copies, waits for them, and re-layouts  3.59 us (2%)
    pallas_call x1, Pallas kernels, rotated_hidden(): pl.pallas_call(functools.partial(hidden_kernel, halvings, doublings, coun...  99.5 us
    pallas_call x1, Pallas kernels, mixed_rows(): pl.pallas_call(functools.partial(down_kernel, levels, folds, span), out_s...  60.4 us
    all_to_all x1, blocking collectives, per_device(): lax.all_to_all(inputs, 'dp', split_axis=1, concat_axis=0, tiled=True)  21.6 us

profile of v2, /device:TPU:0, one launch (start us, length us, event | category | flops | bytes accessed | tf_op | source)
XLA Modules:
  0.0 185.2 jit_solution(862302952241115689)
XLA Ops:
  0.0 1.1 copy.13
  1.1 21.6 %all_to_all.16 = bf16[32,8,1024]{2,0,1:T(8,128)(2,1)S(1)} all-to-all(bf16[32,8,1024]{2,0,1:T(8,128)(2,1)S(1)} %bitcast.17), channel_id=1, replica_groups=mesh['dp'=8,'tensor'=4] {'dp'}, dimensions={1} | all-to-all | bytes 1048576 | tf_op jit(solution)/shard_map/all_to_all | solution.py:419
  22.7 0.8 copy.10
  23.5 99.5 %shard_map.55.refs_0_ = bf16[32,7168]{1,0:T(8,128)(2,1)} custom-call(bf16[256,1024]{1,0:T(8,128)(2,1)} %bitcast.18, bf16[28,1024,256]{2,1,0:T(8,128)(2,1)} %bitcast.13, bf16[28,1024,256]{2,1,0:T(8,128)(2,1)} %bitcast.14, bf16[256,256]{1,0:T(8,128)(2,1)} %constant.2.clone.refs_3_), custom_call_target="tpu_custom_call" | custom-call | flops 7516192768 | bytes 29360128 | tf_op jit(solution)/shard_map/pallas_call | solution.py:218
  123.1 60.4 %shard_map.56 = f32[64,1024]{1,0:T(8,128)} custom-call(bf16[32,7168]{1,0:T(8,128)(2,1)} %shard_map.55.refs_0_, bf16[7168,1024]{1,0:T(8,128)(2,1)} %bitcast.15), custom_call_target="tpu_custom_call" | custom-call | flops 3758096384 | bytes 14680064 | tf_op jit(solution)/shard_map/pallas_call | solution.py:392
  183.5 1.7 copy.15

commit v3 on v2

--- a/solution.py
+++ b/solution.py
@@ -59,19 +59,50 @@
     return me + (1 - 2 * high) * (1 << bit), high
 
 
+def bit_orders(bits, kinds):
+    plain = tuple(range(bits))
+    turned = plain[1:] + plain[:1]
+    return [plain, turned][:kinds]
+
+
+def choose(kind, values):
+    first, second = values
+    return first + kind * (second - first)
+
+
+def place_of(index, order):
+    top = len(order) - 1
+    return sum((index // (1 << bit)) % 2 * (1 << (top - stage)) for stage, bit in enumerate(order))
+
+
 def hidden_kernel(halvings, doublings, factor, *refs):
     x_ref, gate_ref, up_ref, table_ref, out_ref = refs[:5]
     rest = list(refs[5:])
-    weights, part, turned = rest[:3]
-    del rest[:3]
+    columns, weights, part, turned = rest[:4]
+    del rest[:4]
     sends, rest = rest[: halvings + doublings], rest[halvings + doublings :]
     arrivals, rest = rest[: halvings + doublings], rest[halvings + doublings :]
     keeps, rest = rest[:halvings], rest[halvings:]
-    weight_sem, send_sem, recv_sem = rest
-    count, _, block = gate_ref.shape
-    rows = x_ref.shape[0]
-    places = [("dp", bit) + partner_of("dp", bit) for bit in range(halvings)]
-    places += [("tensor", bit) + partner_of("tensor", bit) for bit in range(doublings)]
+    weight_sem, send_sem, recv_sem, own_sem, spread_send_sem, spread_recv_sem = rest
+    count, depth, block = gate_ref.shape
+    own = x_ref.shape[0]
+    groups = 1 << halvings
+    rows = own * groups
+    me = lax.axis_index("dp")
+    orders = bit_orders(halvings, 2)
+    tensor_places = [partner_of("tensor", bit) for bit in range(doublings)]
+    by_bit = [partner_of("dp", bit) for bit in range(halvings)]
+
+    def kind_of(chunk):
+        return lax.rem(chunk, 6) // 5
+
+    def toward(stage, chunk):
+        if stage >= halvings:
+            return "tensor", *tensor_places[stage - halvings]
+        partner, high = (
+            choose(kind_of(chunk), [by_bit[order[stage]][item] for order in orders]) for item in range(2)
+        )
+        return "dp", partner, high
 
     def fetch(chunk, slot):
         return [
@@ -80,7 +111,7 @@
         ]
 
     def transfer(stage, chunk):
-        axis, _, partner, _ = places[stage]
+        axis, partner, _ = toward(stage, chunk)
         return pltpu.make_async_remote_copy(
             src_ref=sends[stage].at[chunk],
             dst_ref=arrivals[stage].at[chunk],
@@ -93,9 +124,38 @@
     for copy in fetch(0, 0):
         copy.start()
     barrier = pltpu.get_barrier_semaphore()
-    for axis, _, partner, _ in places:
-        pl.semaphore_signal(barrier, inc=1, device_id={axis: partner}, device_id_type=pl.DeviceIdType.MESH)
-    pl.semaphore_wait(barrier, len(places))
+    peers = [lax.rem(me + step, groups) for step in range(1, groups)]
+    for peer in peers:
+        pl.semaphore_signal(barrier, inc=1, device_id={"dp": peer}, device_id_type=pl.DeviceIdType.MESH)
+    for partner, _ in tensor_places:
+        pl.semaphore_signal(barrier, inc=1, device_id={"tensor": partner}, device_id_type=pl.DeviceIdType.MESH)
+    mine = columns.at[0, pl.ds(pl.multiple_of(place_of(me, orders[0]) * own, own), own), :]
+
+    def cut(target):
+        return x_ref.at[:, pl.ds(pl.multiple_of(target * depth, depth), depth)]
+
+    kept = pltpu.make_async_copy(cut(me), mine, own_sem)
+    kept.start()
+    pl.semaphore_wait(barrier, len(peers) + doublings)
+    shares = [
+        pltpu.make_async_remote_copy(
+            src_ref=cut(peer),
+            dst_ref=mine,
+            send_sem=spread_send_sem.at[step],
+            recv_sem=spread_recv_sem.at[step],
+            device_id={"dp": peer},
+            device_id_type=pl.DeviceIdType.MESH,
+        )
+        for step, peer in enumerate(peers)
+    ]
+    for share in shares:
+        share.start()
+    kept.wait()
+    for share in shares:
+        share.wait_recv()
+    for index in range(groups):
+        source, target = (place_of(index, order) * own for order in orders)
+        columns[1, target : target + own, :] = columns[0, source : source + own, :]
 
     def multiply(chunk):
         slot = lax.rem(chunk, 2)
@@ -109,10 +169,10 @@
             copy.wait()
         for which in range(2):
             part[:, which * block : (which + 1) * block] = jnp.dot(
-                x_ref[...], weights[slot, which], preferred_element_type=jnp.float32
+                columns[kind_of(chunk)], weights[slot, which], preferred_element_type=jnp.float32
             )
         half = rows // 2
-        high = places[0][3]
+        high = toward(0, chunk)[2]
         theirs = pl.multiple_of((1 - high) * half, half)
         ours = pl.multiple_of(high * half, half)
         sends[0][chunk] = encode(part[pl.ds(theirs, half), :])
@@ -123,7 +183,7 @@
         transfer(stage - 1, chunk).wait_recv()
         slot = lax.rem(chunk, RING)
         half = rows >> (stage + 1)
-        high = places[stage][3]
+        high = toward(stage, chunk)[2]
         theirs = pl.ds(pl.multiple_of((1 - high) * half, half), half)
         ours = pl.ds(pl.multiple_of(high * half, half), half)
         sends[stage][chunk] = encode(keeps[stage - 1][slot, theirs, :] + decode(arrivals[stage - 1][chunk, theirs, :]))
@@ -135,7 +195,6 @@
         both = keeps[halvings - 1][lax.rem(chunk, RING)] + decode(arrivals[halvings - 1][chunk])
         gate, upward = both[:, :block], both[:, block:]
         hidden = gate / (1.0 + jnp.exp(-gate)) * upward
-        own = hidden.shape[0]
         first = hidden.astype(jnp.bfloat16)
         left = hidden - first.astype(jnp.float32)
         second = left.astype(jnp.bfloat16)
@@ -154,7 +213,7 @@
 
     def butterfly(stage, chunk):
         transfer(stage, chunk).wait_recv()
-        sign = (1 - 2 * places[stage][3]).astype(jnp.float32)
+        sign = (1 - 2 * toward(stage, chunk)[2]).astype(jnp.float32)
         store(stage + 1, chunk, sign * sends[stage][chunk] + arrivals[stage][chunk])
 
     steps = [multiply]
@@ -197,17 +256,16 @@
         return carry
 
     lax.fori_loop(0, count, drain, 0)
-
-
-def rotated_hidden(columns, gate_weight, up_weight, groups, tensor):
+    for share in shares:
+        share.wait_send()
+
+
+def rotated_hidden(inputs, gate_weight, up_weight, groups, tensor):
     depth, count, block = gate_weight.shape
-    rows = columns.shape[0]
+    own = inputs.shape[0]
+    rows = own * groups
     halvings = groups.bit_length() - 1
     doublings = tensor.bit_length() - 1
-    own = rows // groups
-    shape = (2,) * halvings + (own, depth)
-    order = tuple(range(halvings))[::-1] + (halvings, halvings + 1)
-    columns = columns.reshape(shape).transpose(order).reshape(rows, depth)
     table = jnp.asarray(sylvester_table(block), jnp.bfloat16)
     halves = [pltpu.VMEM((count, rows >> (level + 1), 2 * block), jnp.bfloat16) for level in range(halvings)]
     wholes = [pltpu.VMEM((count, own, block), jnp.float32) for _ in range(doublings)]
@@ -221,6 +279,7 @@
         in_specs=[vmem, hbm, hbm, vmem],
         out_specs=vmem,
         scratch_shapes=[
+            pltpu.VMEM((2, rows, depth), jnp.bfloat16),
             pltpu.VMEM((2, 2, depth, block), jnp.bfloat16),
             pltpu.VMEM((rows, 2 * block), jnp.float32),
             pltpu.VMEM((count, own, block), jnp.float32),
@@ -232,6 +291,9 @@
             pltpu.SemaphoreType.DMA((2, 2)),
             pltpu.SemaphoreType.DMA((stages, count)),
             pltpu.SemaphoreType.DMA((stages, count)),
+            pltpu.SemaphoreType.DMA,
+            pltpu.SemaphoreType.DMA((groups - 1,)),
+            pltpu.SemaphoreType.DMA((groups - 1,)),
         ],
         compiler_params=pltpu.CompilerParams(collective_id=0, has_side_effects=True, vmem_limit_bytes=56 * 2**20),
         cost_estimate=pl.CostEstimate(
@@ -239,7 +301,7 @@
             bytes_accessed=4 * depth * count * block,
             transcendentals=4 * rows * count * block,
         ),
-    )(columns, jnp.transpose(gate_weight, (1, 0, 2)), jnp.transpose(up_weight, (1, 0, 2)), table)
+    )(inputs, jnp.transpose(gate_weight, (1, 0, 2)), jnp.transpose(up_weight, (1, 0, 2)), table)
 
 
 def reversed_bits(axis, bits):
@@ -416,8 +478,7 @@
 
 def per_device(groups, tensor, inputs, gate_weight, up_weight, down_weight):
     kernel_a, block_e, width = down_weight.shape
-    columns = lax.all_to_all(inputs, "dp", split_axis=1, concat_axis=0, tiled=True)
-    rotated = rotated_hidden(columns, gate_weight, up_weight, groups, tensor)
+    rotated = rotated_hidden(inputs, gate_weight, up_weight, groups, tensor)
     return mixed_rows(rotated, down_weight.reshape(kernel_a * block_e, width), kernel_a, groups, tensor)
 
 

time: 186 us -> 175 us (0.941)
  blocking collectives: 21.6 us -> 0 us
  Pallas kernels: 160 us -> 173 us
  local copies, waits for them, and re-layouts: 3.59 us -> 1.67 us
    all_to_all x1 -> x0, blocking collectives: 21.6 us -> none  [per_device(): lax.all_to_all(inputs, 'dp', split_axis=1, concat_axis=0, tiled=True)]
    pallas_call x1, Pallas kernels: 99.5 us -> 113 us  [rotated_hidden(): pl.pallas_call(functools.partial(hidden_kernel, halvings, doublings, coun...]
where the time goes in v3:
time: 175 us
  Pallas kernels  173 us (99%)
    pallas_call x1, Pallas kernels, rotated_hidden(): pl.pallas_call(functools.partial(hidden_kernel, halvings, doublings, coun...  113 us
    pallas_call x1, Pallas kernels, mixed_rows(): pl.pallas_call(functools.partial(down_kernel, levels, folds, span), out_s...  60.5 us

profile of v3, /device:TPU:0, one launch (start us, length us, event | category | flops | bytes accessed | tf_op | source)
XLA Modules:
  0.0 174.9 jit_solution(3023447352240111876)
XLA Ops:
  0.0 112.7 %shard_map.55.refs_0_ = bf16[32,7168]{1,0:T(8,128)(2,1)} custom-call(bf16[32,8192]{1,0:T(8,128)(2,1)} %refs_0_.1, bf16[28,1024,256]{2,1,0:T(8,128)(2,1)} %bitcast.3, bf16[28,1024,256]{2,1,0:T(8,128)(2,1)} %bitcast.4, bf16[256,256]{1,0:T(8,128)(2,1)} %constant.2.clone.refs_3_), custom_call_target="tpu_custom_call" | custom-call | flops 7516192768 | bytes 29360128 | tf_op jit(solution)/shard_map/pallas_call | solution.py:276
  112.7 60.5 %shard_map.56 = f32[64,1024]{1,0:T(8,128)} custom-call(bf16[32,7168]{1,0:T(8,128)(2,1)} %shard_map.55.refs_0_, bf16[7168,1024]{1,0:T(8,128)(2,1)} %bitcast.5), custom_call_target="tpu_custom_call" | custom-call | flops 3758096384 | bytes 14680064 | tf_op jit(solution)/shard_map/pallas_call | solution.py:454
  173.2 1.7 copy.7

commit v4 on v3

--- a/solution.py
+++ b/solution.py
@@ -10,7 +10,7 @@
 from jax.sharding import PartitionSpec as P
 
 RING = 4
-LAG = 2
+LAG = 3
 
 
 def sylvester_table(order):

time: 175 us -> 171 us (0.977)
  Pallas kernels: 173 us -> 168 us
    pallas_call x1, Pallas kernels: 113 us -> 108 us  [rotated_hidden(): pl.pallas_call(functools.partial(hidden_kernel, halvings, doublings, coun...]
where the time goes in v4:
time: 171 us; the launch traced here: 170 us
  Pallas kernels  168 us (98%)
    pallas_call x1, Pallas kernels, rotated_hidden(): pl.pallas_call(functools.partial(hidden_kernel, halvings, doublings, coun...  108 us
    pallas_call x1, Pallas kernels, mixed_rows(): pl.pallas_call(functools.partial(down_kernel, levels, folds, span), out_s...  60.4 us

profile of v4, /device:TPU:0, one launch (start us, length us, event | category | flops | bytes accessed | tf_op | source)
XLA Modules:
  0.0 169.7 jit_solution(17403461666167049496)
XLA Ops:
  0.0 107.6 %shard_map.55.refs_0_ = bf16[32,7168]{1,0:T(8,128)(2,1)} custom-call(bf16[32,8192]{1,0:T(8,128)(2,1)} %refs_0_.1, bf16[28,1024,256]{2,1,0:T(8,128)(2,1)} %bitcast.3, bf16[28,1024,256]{2,1,0:T(8,128)(2,1)} %bitcast.4, bf16[256,256]{1,0:T(8,128)(2,1)} %constant.2.clone.refs_3_), custom_call_target="tpu_custom_call" | custom-call | flops 7516192768 | bytes 29360128 | tf_op jit(solution)/shard_map/pallas_call | solution.py:276
  107.6 60.4 %shard_map.56 = f32[64,1024]{1,0:T(8,128)} custom-call(bf16[32,7168]{1,0:T(8,128)(2,1)} %shard_map.55.refs_0_, bf16[7168,1024]{1,0:T(8,128)(2,1)} %bitcast.5), custom_call_target="tpu_custom_call" | custom-call | flops 3758096384 | bytes 14680064 | tf_op jit(solution)/shard_map/pallas_call | solution.py:454
  168.0 1.7 copy.7
